TPU v7x, 32 devices: a whole 2x2x4 slice. The times are simulated.
32 devices in a mesh: groups: 2 (over x), ctx: 16 (over z, y, core).
Axes of the slice: x: 2, y: 2, z: 4, core: 2. Of those that a mesh axis runs over, the one named last changes fastest.
Arguments:
- queries: bfloat16 [8192, 2048], P(('groups', 'ctx')), parts along dimension 0, may hold values from -6 to 6
- keys: bfloat16 [8192, 2048], P(('groups', 'ctx')), parts along dimension 0, may hold values from -5 to 5
- values: bfloat16 [8192, 2048], P(('groups', 'ctx')), parts along dimension 0, may hold values from -6 to 6
- bar_lengths: int32 [32], P('groups'), parts along dimension 0, may hold values from 32 to 256, as said below
Outputs:
- attended: bfloat16 [8192, 2048], P(('groups', 'ctx')), parts along dimension 0
There are 2 independent parts, one for each index of `groups`. A program takes and returns all parts, laid end to end along the dimension named above; each array names one. Nothing has to cross between parts.
Inputs may be any that keep to these rules, and one draw needn't show every extreme that they name: `bar_lengths`: used tokens of each bar; the rest of its 256 slots are padding.
All inputs are finite; a program needn't handle non-finite values.
Results may differ from a plain program's by a relative error of at most 0.0038.
Values may be sent and summed in bfloat16 or wider, within the bound.
A program may use at most 128 MiB of HBM per device.

v0:
```python
import math

import jax
import jax.numpy as jnp
from jax import lax
from jax.sharding import PartitionSpec as P

HD = 128


BAR_OFFSETS = (1, 2, 4, 8, 12, 16, 24, 32)
NEG_FILL = -1e30


def from_behind(value, axis, steps):
    count = lax.axis_size(axis)
    initial, last = (max(0, -steps), min(count, count - steps))
    return lax.ppermute(value, axis, [(source, source + steps) for source in range(initial, last)])


def local(queries, keys, values, bar_lengths):
    axis_count = lax.axis_size("ctx")
    this_bar = lax.axis_index("ctx")
    bar_rows = queries.shape[0]
    features = queries.shape[1]
    head_count = features // HD
    positions = jnp.arange(bar_rows, dtype=jnp.int32)
    own_len = bar_lengths[this_bar]
    live_rows = (positions < own_len).astype(jnp.bfloat16)[None, :]
    factor = lax.rsqrt(own_len.astype(jnp.float32))
    pooled_keys = (jnp.dot(live_rows, keys, preferred_element_type=jnp.float32) * factor).astype(
        jnp.bfloat16
    )
    pooled_values = (
        jnp.dot(live_rows, values, preferred_element_type=jnp.float32) * factor
    ).astype(jnp.bfloat16)
    summary_keys, summary_values = (
        lax.all_gather(pooled_keys, "ctx", axis=0, tiled=True),
        lax.all_gather(pooled_values, "ctx", axis=0, tiled=True),
    )
    offsets_used = [offset for offset in BAR_OFFSETS if offset < axis_count]
    stacked = jnp.stack([keys, values])
    fetched = []
    for offset in offsets_used:
        fetched.append(from_behind(stacked, "ctx", offset))
    key_parts = [keys]
    value_parts = [values]
    mask_parts = [(positions[None, :] <= positions[:, None]) & (positions[None, :] < own_len)]
    for offset, arrived in zip(offsets_used, fetched):
        source_bar = this_bar - offset
        clamped = jnp.maximum(source_bar, 0)
        near_len = jnp.where(source_bar >= 0, bar_lengths[clamped], 0)
        key_parts.append(arrived[0])
        value_parts.append(arrived[1])
        mask_parts.append(jnp.broadcast_to((positions < near_len)[None, :], (bar_rows, bar_rows)))
    all_bars = jnp.arange(axis_count, dtype=jnp.int32)
    coarse = all_bars < this_bar
    for offset in BAR_OFFSETS:
        coarse = coarse & (all_bars != this_bar - offset)
    key_parts.append(summary_keys)
    value_parts.append(summary_values)
    mask_parts.append(jnp.broadcast_to(coarse[None, :], (bar_rows, axis_count)))
    key_rows = jnp.concatenate(key_parts, 0).reshape(-1, head_count, HD)
    value_rows = jnp.concatenate(value_parts, 0).reshape(-1, head_count, HD)
    key_mask = jnp.concatenate(mask_parts, 1)
    query_heads = queries.reshape(bar_rows, head_count, HD)
    scores = jnp.einsum(
        "qhd,khd->hqk", query_heads, key_rows, preferred_element_type=jnp.float32
    ) * (1.0 / math.sqrt(HD))
    scores = jnp.where(key_mask[None], scores, NEG_FILL)
    row_max = jnp.max(scores, axis=2, keepdims=True)
    weights = jnp.where(key_mask[None], jnp.exp(scores - row_max), 0.0)
    row_total = jnp.sum(weights, axis=2)
    rounded = weights.astype(jnp.bfloat16)
    mixed = jnp.einsum("hqk,khd->qhd", rounded, value_rows, preferred_element_type=jnp.float32)
    mixed = mixed / jnp.transpose(row_total)[:, :, None]
    mixed = mixed * (positions < own_len).astype(jnp.float32)[:, None, None]
    return mixed.reshape(bar_rows, features).astype(jnp.bfloat16)


def solution(mesh):
    placed = (
        P(("groups", "ctx"), None),
        P(("groups", "ctx"), None),
        P(("groups", "ctx"), None),
        P("groups"),
    )
    return jax.shard_map(
        local, mesh=mesh, in_specs=placed, out_specs=P(("groups", "ctx"), None), check_vma=False
    )
```

profile of v0, /device:TPU:26, one launch (start us, length us, event | category | flops | bytes accessed | tf_op | source)
XLA Modules:
  0.0 357.9 jit_solution(13986242170819703529)
XLA Ops:
  0.0 1.6 copy.27
  1.6 1.5 copy.28
  3.1 1.5 pad_maximum_fusion
  4.6 1.9 collective-permute-start
  6.5 3.4 collective-permute-start.1
  9.9 1.3 collective-permute-start.2
  11.2 1.3 collective-permute-start.3
  12.5 1.3 collective-permute-start.4
  13.8 0.7 fusion.32
  14.5 0.6 iota_compare_fusion.6
  15.9 0.1 fusion.23
  16.0 1.2 fusion.26
  17.2 1.3 copy.30
  18.5 2.6 constant_dynamic-update-slice_fusion.5
  21.1 1.5 fusion.36
  23.3 0.6 iota_compare_fusion.5
  24.5 0.6 iota_compare_fusion.4
  25.7 0.5 iota_compare_fusion.3
  26.8 0.5 iota_compare_fusion.2
  27.3 1.3 copy.38
  28.6 2.5 constant_dynamic-update-slice_fusion.12
  31.1 0.8 broadcast_dynamic-update-slice_fusion.4
  32.5 0.8 broadcast_dynamic-update-slice_fusion.3
  33.3 0.7 broadcast_dynamic-update-slice_fusion.2
  34.1 0.9 fusion.37
  35.0 0.7 broadcast_dynamic-update-slice_fusion.1
  35.7 0.8 copy-done.11
  36.5 227.8 %all-gather = bf16[32768]{0:T(1024)(128)(2,1)S(1)} all-gather(bf16[2048]{0:T(1024)(128)(2,1)S(1)} %multiply_convert_fusion.1), channel_id=2, replica_groups=mesh['groups'=2,'ctx'=16] {'ctx'}, dimensions={0}, use_global_device_ids=true | all-gather | bytes 69632 | tf_op jit(solution)/shard_map/all_gather | solution.py:39
  264.3 15.8 %all-gather.1 = bf16[32768]{0:T(1024)(128)(2,1)S(1)} all-gather(bf16[2048]{0:T(1024)(128)(2,1)S(1)} %multiply_convert_fusion), channel_id=3, replica_groups=mesh['groups'=2,'ctx'=16] {'ctx'}, dimensions={0}, use_global_device_ids=true | all-gather | bytes 69632 | tf_op jit(solution)/shard_map/all_gather | solution.py:38
  280.1 0.7 broadcast_dynamic-update-slice_fusion
  280.8 0.7 constant_dynamic-update-slice_fusion.6
  281.5 0.0 collective-permute-done
  281.5 2.6 fusion.31
  284.2 0.7 copy.31
  284.8 3.1 fusion.30
  287.9 1.6 copy.32
  289.5 3.0 fusion.29
  292.6 2.3 copy.33
  294.8 0.0 collective-permute-done.3
  294.8 3.0 fusion.28
  297.8 2.3 copy.34
  300.1 0.0 collective-permute-done.4
  300.1 3.0 fusion.27
  303.1 2.3 copy.35
  305.3 2.3 copy.39
  307.6 2.3 copy.40
  309.8 2.3 copy.41
  312.1 2.3 copy.42
  314.4 2.3 copy.43
  316.7 1.2 constant_dynamic-update-slice_fusion.4
  317.9 1.2 constant_dynamic-update-slice_fusion.3
  319.1 2.6 constant_dynamic-update-slice_fusion.2
  321.7 1.2 constant_dynamic-update-slice_fusion.1
  322.9 1.2 constant_dynamic-update-slice_fusion
  324.1 0.6 copy_dynamic-update-slice_fusion.1
  324.7 1.1 constant_dynamic-update-slice_fusion.11
  325.9 1.2 constant_dynamic-update-slice_fusion.10
  327.1 1.2 constant_dynamic-update-slice_fusion.9
  328.3 1.2 constant_dynamic-update-slice_fusion.8
  329.5 1.2 constant_dynamic-update-slice_fusion.7
  330.7 0.7 copy_dynamic-update-slice_fusion
  331.3 16.2 %fusion.33 = (f32[16,256]{1,0:T(8,128)S(1)}, bf16[16,256,1552]{1,2,0:T(8,128)(2,1)}) fusion(pred[256,1552]{0,1:T(8,128)(4,1)S(1)} %copy-done.12, bf16[1552,16,128]{2,0,1:T(8,128)(2,1)} %copy_dynamic-update-slice_fusion, bf16[256,2048]{1,0:T(8,128)(2,1)S(1)} %copy-done), kind=kOutput, calls=%fused_computation.60 | convolution fusion | flops 1665533440 | bytes 20533248 | tf_op jit(solution)/shard_map/sub | solution.py:72
  347.5 9.0 %fusion.10 = bf16[256,16,128]{0,2,1:T(8,128)(2,1)S(1)} fusion(bf16[1552,16,128]{2,0,1:T(8,128)(2,1)} %copy_dynamic-update-slice_fusion.1, bf16[16,256,1552]{1,2,0:T(8,128)(2,1)} %get-tuple-element.22, f32[256]{0:T(256)S(1)} %copy-done.14, f32[256,16]{0,1:T(8,128)S(1)} %bitcast.80), kind=kOutput, calls=%fused_computation.13 | convolution fusion | flops 1628962816 | bytes 20136960 | tf_op jit(solution)/shard_map/hqk,khd->qhd/dot_general | solution.py:75
  356.5 1.4 copy.46
  (36 shorter events, 0.1 us)
Async XLA Ops:
  0.0 331.3 %copy-start = (bf16[256,2048]{1,0:T(8,128)(2,1)S(1)}, bf16[256,2048]{1,0:T(8,128)(2,1)}, u32[]{:S(2)}) copy-start(bf16[256,2048]{1,0:T(8,128)(2,1)} %param.4) | copy-start | bytes 3145732
  0.0 13.8 %copy-start.10 = (s32[16]{0:T(128)S(1)}, s32[16]{0:T(128)}, u32[]{:S(2)}) copy-start(s32[16]{0:T(128)} %param.7) | copy-start | bytes 196
  4.6 277.0 %collective-permute-start = (bf16[2,256,2048]{1,2,0:T(8,128)(2,1)}, bf16[2,256,2048]{1,2,0:T(8,128)(2,1)}, u32[]{:S(2)}, u32[]{:S(2)}) collective-permute-start(bf16[2,256,2048]{1,2,0:T(8,128)(2,1)} %pad_maximum_fusion), channel_id=1, source_target_pairs={{0,1},{1,2},{2,3},{3,4},{4,5},{5,6},{6,7},{7,8},{8,9},{9,10},{10,1... | collective-permute-start | bytes 6291464 | tf_op jit(solution)/shard_map/ppermute | solution.py:18
  6.5 278.4 %collective-permute-start.1 = (bf16[2,256,2048]{1,2,0:T(8,128)(2,1)}, bf16[2,256,2048]{1,2,0:T(8,128)(2,1)}, u32[]{:S(2)}, u32[]{:S(2)}) collective-permute-start(bf16[2,256,2048]{1,2,0:T(8,128)(2,1)} %pad_maximum_fusion), channel_id=1, source_target_pairs={{0,2},{1,3},{2,4},{3,5},{4,6},{5,7},{6,8},{7,9},{8,10},{9,11},{10,... | collective-permute-start | bytes 6291464 | tf_op jit(solution)/shard_map/ppermute | solution.py:18
  9.9 279.6 %collective-permute-start.2 = (bf16[2,256,2048]{1,2,0:T(8,128)(2,1)}, bf16[2,256,2048]{1,2,0:T(8,128)(2,1)}, u32[]{:S(2)}, u32[]{:S(2)}) collective-permute-start(bf16[2,256,2048]{1,2,0:T(8,128)(2,1)} %pad_maximum_fusion), channel_id=1, source_target_pairs={{0,4},{1,5},{2,6},{3,7},{4,8},{5,9},{6,10},{7,11},{8,12},{9,13},{1... | collective-permute-start | bytes 6291464 | tf_op jit(solution)/shard_map/ppermute | solution.py:18
  11.2 283.6 %collective-permute-start.3 = (bf16[2,256,2048]{1,2,0:T(8,128)(2,1)}, bf16[2,256,2048]{1,2,0:T(8,128)(2,1)}, u32[]{:S(2)}, u32[]{:S(2)}) collective-permute-start(bf16[2,256,2048]{1,2,0:T(8,128)(2,1)} %pad_maximum_fusion), channel_id=1, source_target_pairs={{0,8},{1,9},{2,10},{3,11},{4,12},{5,13},{6,14},{7,15},{16,24},{17,... | collective-permute-start | bytes 6291464 | tf_op jit(solution)/shard_map/ppermute | solution.py:18
  12.5 287.6 %collective-permute-start.4 = (bf16[2,256,2048]{1,2,0:T(8,128)(2,1)}, bf16[2,256,2048]{1,2,0:T(8,128)(2,1)}, u32[]{:S(2)}, u32[]{:S(2)}) collective-permute-start(bf16[2,256,2048]{1,2,0:T(8,128)(2,1)} %pad_maximum_fusion), channel_id=1, source_target_pairs={{0,12},{1,13},{2,14},{3,15},{16,28},{17,29},{18,30},{19,31}} | collective-permute-start | bytes 6291464 | tf_op jit(solution)/shard_map/ppermute | solution.py:18
  15.8 16.7 %copy-start.13 = (pred[256,1]{0,1:T(4,128)(4,1)}, pred[256,1]{0,1:T(4,128)(4,1)S(1)}, u32[]{:S(2)}) copy-start(pred[256,1]{0,1:T(4,128)(4,1)S(1)} %reshape.106) | copy-start | bytes 772
  18.5 15.5 %copy-start.2 = (bf16[256,2048]{1,0:T(8,128)(2,1)S(1)}, bf16[256,2048]{1,0:T(8,128)(2,1)}, u32[]{:S(2)}) copy-start(bf16[256,2048]{1,0:T(8,128)(2,1)} %param.5) | copy-start | bytes 3145732
  35.7 0.8 copy-start.11
  316.6 5.0 %copy-start.3 = (bf16[256,16,128]{2,0,1:T(8,128)(2,1)S(1)}, bf16[256,16,128]{2,0,1:T(8,128)(2,1)}, u32[]{:S(2)}) copy-start(bf16[256,16,128]{2,0,1:T(8,128)(2,1)} %copy.34) | copy-start | bytes 3145732
  316.7 6.3 %copy-start.9 = (bf16[256,16,128]{2,0,1:T(8,128)(2,1)S(1)}, bf16[256,16,128]{2,0,1:T(8,128)(2,1)}, u32[]{:S(2)}) copy-start(bf16[256,16,128]{2,0,1:T(8,128)(2,1)} %copy.35) | copy-start | bytes 3145732
  316.7 8.1 %copy-start.4 = (bf16[256,16,128]{2,0,1:T(8,128)(2,1)S(1)}, bf16[256,16,128]{2,0,1:T(8,128)(2,1)}, u32[]{:S(2)}) copy-start(bf16[256,16,128]{2,0,1:T(8,128)(2,1)} %copy.39) | copy-start | bytes 3145732
  316.7 9.2 %copy-start.5 = (bf16[256,16,128]{2,0,1:T(8,128)(2,1)S(1)}, bf16[256,16,128]{2,0,1:T(8,128)(2,1)}, u32[]{:S(2)}) copy-start(bf16[256,16,128]{2,0,1:T(8,128)(2,1)} %copy.40) | copy-start | bytes 3145732
  317.9 9.2 %copy-start.6 = (bf16[256,16,128]{2,0,1:T(8,128)(2,1)S(1)}, bf16[256,16,128]{2,0,1:T(8,128)(2,1)}, u32[]{:S(2)}) copy-start(bf16[256,16,128]{2,0,1:T(8,128)(2,1)} %copy.41) | copy-start | bytes 3145732
  319.1 9.2 %copy-start.7 = (bf16[256,16,128]{2,0,1:T(8,128)(2,1)S(1)}, bf16[256,16,128]{2,0,1:T(8,128)(2,1)}, u32[]{:S(2)}) copy-start(bf16[256,16,128]{2,0,1:T(8,128)(2,1)} %copy.42) | copy-start | bytes 3145732
  321.7 7.8 %copy-start.8 = (bf16[256,16,128]{2,0,1:T(8,128)(2,1)S(1)}, bf16[256,16,128]{2,0,1:T(8,128)(2,1)}, u32[]{:S(2)}) copy-start(bf16[256,16,128]{2,0,1:T(8,128)(2,1)} %copy.43) | copy-start | bytes 3145732
  322.9 8.4 %copy-start.12 = (pred[256,1552]{0,1:T(8,128)(4,1)S(1)}, pred[256,1552]{0,1:T(8,128)(4,1)}, u32[]{:S(2)}) copy-start(pred[256,1552]{0,1:T(8,128)(4,1)} %constant_dynamic-update-slice_fusion.6) | copy-start | bytes 1191940
  331.3 16.2 %copy-start.14 = (f32[256]{0:T(256)S(1)}, f32[256]{0:T(256)}, u32[]{:S(2)}) copy-start(f32[256]{0:T(256)} %fusion.26) | copy-start | bytes 3076
  347.5 10.4 %copy-start.1 = (bf16[256,2048]{1,0:T(8,128)(2,1)S(1)}, bf16[256,2048]{1,0:T(8,128)(2,1)}, u32[]{:S(2)}) copy-start(bf16[256,2048]{1,0:T(8,128)(2,1)} %param.4) | copy-start | bytes 3145732
where the time goes:
time: 365 us; the launch traced here: 358 us
  blocking collectives  244 us (67%)
  local copies, waits for them, and re-layouts  67.8 us (19%)
  matrix products  27.5 us (8%)
  starting transfers between devices  9.21 us (3%)
  other arithmetic  5.7 us (2%)
  between operations  4.11 us (1%)
    all_gather x1, blocking collectives, local(): lax.all_gather(pooled_values, 'ctx', axis=0, tiled=True)  228 us
    unnamed x49, local copies, waits for them, and re-layouts  26 us
    sub x1, matrix products, local(): weights = jnp.where(key_mask[None], jnp.exp(scores - row_max), 0.0)  16.2 us
    all_gather x1, blocking collectives, local(): lax.all_gather(pooled_keys, 'ctx', axis=0, tiled=True)  15.8 us
    slice x5, local copies, waits for them, and re-layouts, local(): key_parts.append(arrived[0])  14.7 us
    concatenate x7, local copies, waits for them, and re-layouts, local(): key_rows = jnp.concatenate(key_parts, 0).reshape(-1, head_count, HD)  13.3 us
    concatenate x7, local copies, waits for them, and re-layouts, local(): value_rows = jnp.concatenate(value_parts, 0).reshape(-1, head_count, HD)  11 us
    ppermute x5, starting transfers between devices, from_behind(): lax.ppermute(value, axis, [(source, source + steps) for source in range(i...  9.21 us
  transfers between devices with their start and end apart: 5, of which 0 were waited for; matrix products, arithmetic and copies ran while one was open for 11% of the time, Pallas kernels for 0%

commit v1 on v0

v1 whole, which is shorter than its diff:
```python
import functools
import math

import jax
import jax.numpy as jnp
from jax import lax
from jax.experimental import pallas as pl
from jax.experimental.pallas import tpu as pltpu
from jax.sharding import PartitionSpec as P

HD = 128
BAR_OFFSETS = (1, 2, 4, 8, 12, 16, 24, 32)
NEG_FILL = -1e30
LOG2E = math.log2(math.e)
SCALE = LOG2E / math.sqrt(HD)
CHUNKS = 4
AHEAD = 1
STRIDE = 4


def kernel(
    nb, hops, chunks, len_ref, q_ref, k_ref, v_ref, o_ref,
    qin, oin, osend, lin, lsend, acc, mst, lst, sum_f32, sum_send, sum_in, sum_wide, sum_rows,
    q_send, q_recv, o_send, o_recv, l_send, l_recv, s_send, s_recv,
):
    rows, features = q_ref.shape
    heads = features // HD
    width = features // chunks
    per = width // HD
    near2, near1 = hops, hops + 1
    slots = hops + 2
    me = lax.axis_index("ctx")
    low_half = lax.rem(lax.div(me, 2), 2) == 0
    even = lax.rem(me, 2) == 0
    own_len = len_ref[me]

    def columns(c):
        return pl.ds(pl.multiple_of(c * width, width), width)

    def exists(slot):
        far = me + STRIDE * (slot + 1) < nb
        return jnp.where(slot == near2, me + 2 < nb, jnp.where(slot == near1, me + 1 < nb, far))

    def parent(slot):
        two = jnp.where(low_half, me + 2, me - 2)
        one = jnp.where(even, me + 1, me - 1)
        return jnp.where(slot == near2, two, jnp.where(slot == near1, one, me + STRIDE))

    def q_copy(src, slot, c, target):
        return pltpu.make_async_remote_copy(
            src_ref=src, dst_ref=qin.at[slot, c], send_sem=q_send.at[slot, c],
            recv_sem=q_recv.at[slot, c], device_id={"ctx": target},
            device_id_type=pl.DeviceIdType.MESH,
        )

    def o_copies(slot, c, target):
        return (
            pltpu.make_async_remote_copy(
                src_ref=osend.at[slot, c], dst_ref=oin.at[slot, c], send_sem=o_send.at[slot, c],
                recv_sem=o_recv.at[slot, c], device_id={"ctx": target},
                device_id_type=pl.DeviceIdType.MESH,
            ),
            pltpu.make_async_remote_copy(
                src_ref=lsend.at[slot, c], dst_ref=lin.at[slot, c], send_sem=l_send.at[slot, c],
                recv_sem=l_recv.at[slot, c], device_id={"ctx": target},
                device_id_type=pl.DeviceIdType.MESH,
            ),
        )

    def s_copy(target):
        return pltpu.make_async_remote_copy(
            src_ref=sum_send, dst_ref=sum_in.at[me], send_sem=s_send.at[target],
            recv_sem=s_recv.at[me], device_id={"ctx": target},
            device_id_type=pl.DeviceIdType.MESH,
        )

    sum_in[...] = jnp.zeros_like(sum_in)
    barrier = pltpu.get_barrier_semaphore()

    @pl.loop(0, nb)
    def _(j):
        @pl.when(j != me)
        def _():
            pl.semaphore_signal(
                barrier, inc=1, device_id={"ctx": j}, device_id_type=pl.DeviceIdType.MESH
            )

    live = (lax.broadcasted_iota(jnp.int32, (16, rows), 1) < own_len).astype(jnp.bfloat16)
    factor = lax.rsqrt(jnp.full((1, HD), own_len, jnp.int32).astype(jnp.float32))
    for part, ref in enumerate((k_ref, v_ref)):
        for h in range(heads):
            pooled = jnp.dot(
                live, ref[:, h * HD : (h + 1) * HD], preferred_element_type=jnp.float32
            )
            sum_f32[part * heads + h : part * heads + h + 1, :] = pooled[0:1, :] * factor
    sum_send[...] = sum_f32[...].astype(jnp.bfloat16)

    pl.semaphore_wait(barrier, nb - 1)

    for c in range(chunks):
        source = q_ref.at[:, c * width : (c + 1) * width]

        @pl.when(me >= STRIDE)
        def _():
            q_copy(source, 0, c, me - STRIDE).start()

        @pl.when(jnp.logical_not(low_half))
        def _():
            q_copy(source, near2, c, me - 2).start()

        @pl.when(jnp.logical_not(even))
        def _():
            q_copy(source, near1, c, me - 1).start()

        if c == 0:
            @pl.loop(0, nb)
            def _(j):
                @pl.when(j > me)
                def _():
                    s_copy(j).start()

    def forward(c):
        for slot in range(slots):
            @pl.when(exists(slot))
            def _(slot=slot):
                q_copy(qin.at[slot, c], slot, c, parent(slot)).wait_recv()
                if slot + 1 < hops:
                    @pl.when(me >= STRIDE)
                    def _():
                        q_copy(qin.at[slot, c], slot + 1, c, me - STRIDE).start()
                if slot == 0:
                    @pl.when(low_half)
                    def _():
                        q_copy(qin.at[slot, c], near2, c, me + 2).start()
                if slot == near2:
                    @pl.when(even)
                    def _():
                        q_copy(qin.at[slot, c], near1, c, me + 1).start()

    lane = lax.broadcasted_iota(jnp.int32, (rows, HD), 1)
    key_pos = lax.broadcasted_iota(jnp.int32, (1, rows), 1)
    live_bias = jnp.where(key_pos < own_len, 0.0, NEG_FILL).astype(jnp.float32)

    def scores_of(q, k):
        return lax.dot_general(
            q, k, (((1,), (1,)), ((), ())), preferred_element_type=jnp.float32
        ) * SCALE

    def head_columns(c, h):
        return pl.ds(pl.multiple_of(c * width + h * HD, HD), HD)

    def local_peer(slot, c):
        m_all = jnp.zeros((rows, HD), jnp.float32)
        l_all = jnp.ones((rows, HD), jnp.float32)
        for h in range(per):
            here = slice(h * HD, (h + 1) * HD)
            s = scores_of(qin[slot, c, :, here], k_ref[:, head_columns(c, h)]) + live_bias
            m = jnp.max(s, axis=1, keepdims=True)
            p = jnp.exp2(s - m)
            l = jnp.sum(p, axis=1, keepdims=True)
            acc[:, here] = jnp.dot(
                p.astype(jnp.bfloat16), v_ref[:, head_columns(c, h)],
                preferred_element_type=jnp.float32,
            )
            m_all = jnp.where(lane == h, m, m_all)
            l_all = jnp.where(lane == h, l, l_all)
        mst[...] = m_all
        lst[...] = l_all

    def local_own(c):
        causal = (
            lax.broadcasted_iota(jnp.int32, (rows, rows), 1)
            <= lax.broadcasted_iota(jnp.int32, (rows, rows), 0)
        ) & (key_pos < own_len)
        bars = lax.broadcasted_iota(jnp.int32, (1, nb), 1)
        coarse = bars < me
        for offset in BAR_OFFSETS:
            coarse = coarse & (bars != me - offset)
        coarse_bias = jnp.where(coarse, 0.0, NEG_FILL).astype(jnp.float32)
        m_all = jnp.zeros((rows, HD), jnp.float32)
        l_all = jnp.ones((rows, HD), jnp.float32)
        for h in range(per):
            here = slice(h * HD, (h + 1) * HD)
            q = q_ref[:, head_columns(c, h)]
            s = jnp.where(causal, scores_of(q, k_ref[:, head_columns(c, h)]), NEG_FILL)
            t = scores_of(q, sum_rows[0, :, head_columns(c, h)]) + coarse_bias
            m = jnp.maximum(
                jnp.max(s, axis=1, keepdims=True), jnp.max(t, axis=1, keepdims=True)
            )
            p = jnp.exp2(s - m)
            r = jnp.exp2(t - m)
            l = jnp.sum(p, axis=1, keepdims=True) + jnp.sum(r, axis=1, keepdims=True)
            acc[:, here] = jnp.dot(
                p.astype(jnp.bfloat16), v_ref[:, head_columns(c, h)],
                preferred_element_type=jnp.float32,
            ) + jnp.dot(
                r.astype(jnp.bfloat16), sum_rows[1, :, head_columns(c, h)],
                preferred_element_type=jnp.float32,
            )
            m_all = jnp.where(lane == h, m, m_all)
            l_all = jnp.where(lane == h, l, l_all)
        mst[...] = m_all
        lst[...] = l_all

    def merge(slot, c):
        for copy in o_copies(slot, c, parent(slot)):
            copy.wait_recv()
        padded = jnp.concatenate(
            [lin[slot, c], jnp.zeros((HD - lin.shape[2], rows), jnp.float32)], axis=0
        )
        theirs = jnp.transpose(padded)
        mine = mst[...]
        top = jnp.maximum(mine, theirs)
        keep = jnp.exp2(mine - top)
        add = jnp.exp2(theirs - top)
        mst[...] = top
        lst[...] = lst[...] * keep + add
        for h in range(per):
            here = slice(h * HD, (h + 1) * HD)
            acc[:, here] = (
                acc[:, here] * keep[:, h : h + 1]
                + oin[slot, c, :, here].astype(jnp.float32) * add[:, h : h + 1]
            )

    idle_hops = [s for s in range(hops) if STRIDE * (s + 1) not in BAR_OFFSETS]

    def answer(slot, c):
        if idle_hops:
            idle = functools.reduce(jnp.logical_or, [slot == s for s in idle_hops])

            @pl.when(idle)
            def _():
                acc[...] = jnp.zeros_like(acc)
                mst[...] = jnp.full_like(mst, NEG_FILL)
                lst[...] = jnp.ones_like(lst)

            @pl.when(jnp.logical_not(idle))
            def _():
                local_peer(slot, c)
        else:
            local_peer(slot, c)

        @pl.when((slot + 1 < hops) & (me >= STRIDE))
        def _():
            merge(jnp.minimum(slot + 1, hops - 1), c)

        @pl.when((slot == 0) & low_half)
        def _():
            merge(near2, c)

        @pl.when((slot == near2) & even)
        def _():
            merge(near1, c)

        total = lst[...]
        inverse = 1.0 / total
        for h in range(per):
            here = slice(h * HD, (h + 1) * HD)
            osend[slot, c, :, here] = (acc[:, here] * inverse[:, h : h + 1]).astype(jnp.bfloat16)
        level = mst[...] + jnp.log(total) * LOG2E
        lsend[slot, c] = jnp.transpose(level)[: lsend.shape[2], :]
        for copy in o_copies(slot, c, parent(slot)):
            copy.start()

    def finish(c):
        local_own(c)

        @pl.when(me >= STRIDE)
        def _():
            merge(0, c)

        @pl.when(jnp.logical_not(low_half))
        def _():
            merge(near2, c)

        @pl.when(jnp.logical_not(even))
        def _():
            merge(near1, c)

        used = lax.broadcasted_iota(jnp.int32, (rows, HD), 0) < own_len
        inverse = jnp.where(used, 1.0 / lst[...], 0.0)
        for h in range(per):
            o_ref[:, head_columns(c, h)] = (
                acc[:, h * HD : (h + 1) * HD] * inverse[:, h : h + 1]
            ).astype(o_ref.dtype)

    for c in range(min(AHEAD, chunks)):
        forward(c)

    @pl.loop(0, nb)
    def _(j):
        @pl.when(j < me)
        def _():
            pltpu.make_async_remote_copy(
                src_ref=sum_send, dst_ref=sum_in.at[j], send_sem=s_send.at[j],
                recv_sem=s_recv.at[j], device_id={"ctx": j},
                device_id_type=pl.DeviceIdType.MESH,
            ).wait_recv()

    sum_wide[...] = sum_in[...].astype(jnp.float32)
    for part in range(2):
        for h in range(heads):
            sum_rows[part, :, h * HD : (h + 1) * HD] = sum_wide[:, part * heads + h, :].astype(
                jnp.bfloat16
            )

    @pl.loop(0, chunks + 1)
    def _(step):
        @pl.when(step + AHEAD < chunks)
        def _():
            forward(step + AHEAD)

        @pl.when(step < chunks)
        def _():
            @pl.loop(0, slots)
            def _(j):
                slot = slots - 1 - j

                @pl.when(exists(slot))
                def _():
                    answer(slot, step)

        @pl.when(step >= 1)
        def _():
            finish(step - 1)

    @pl.loop(0, nb)
    def _(j):
        @pl.when(j > me)
        def _():
            s_copy(j).wait_send()

    @pl.loop(0, chunks)
    def _(c):
        for slot in range(slots):
            if slot == 0:
                sent = me >= STRIDE
            elif slot < hops:
                sent = (me >= STRIDE) & (me + STRIDE * slot < nb)
            elif slot == near2:
                sent = jnp.logical_not(low_half) | (me + STRIDE < nb)
            else:
                sent = jnp.logical_not(even) | (me + 2 < nb)

            @pl.when(sent)
            def _(slot=slot):
                q_copy(qin.at[slot, c], slot, c, parent(slot)).wait_send()

            @pl.when(exists(slot))
            def _(slot=slot):
                for copy in o_copies(slot, c, parent(slot)):
                    copy.wait_send()


def local(queries, keys, values, bar_lengths):
    nb = lax.axis_size("ctx")
    rows, features = queries.shape
    heads = features // HD
    chunks = CHUNKS
    width = features // chunks
    hops = max(o // STRIDE for o in BAR_OFFSETS if o % STRIDE == 0 and o < nb)
    slots = hops + 2
    stat_rows = 8
    piece = (slots, chunks, rows, width)
    sems = pltpu.SemaphoreType.DMA((slots, chunks))
    whole = pl.BlockSpec(memory_space=pltpu.VMEM)
    return pl.pallas_call(
        functools.partial(kernel, nb, hops, chunks),
        out_shape=jax.ShapeDtypeStruct((rows, features), jnp.bfloat16),
        in_specs=[pl.BlockSpec(memory_space=pltpu.SMEM), whole, whole, whole],
        out_specs=whole,
        scratch_shapes=[
            pltpu.VMEM(piece, jnp.bfloat16),
            pltpu.VMEM(piece, jnp.bfloat16),
            pltpu.VMEM(piece, jnp.bfloat16),
            pltpu.VMEM((slots, chunks, stat_rows, rows), jnp.float32),
            pltpu.VMEM((slots, chunks, stat_rows, rows), jnp.float32),
            pltpu.VMEM((rows, width), jnp.float32),
            pltpu.VMEM((rows, HD), jnp.float32),
            pltpu.VMEM((rows, HD), jnp.float32),
            pltpu.VMEM((2 * heads, HD), jnp.float32),
            pltpu.VMEM((2 * heads, HD), jnp.bfloat16),
            pltpu.VMEM((nb, 2 * heads, HD), jnp.bfloat16),
            pltpu.VMEM((nb, 2 * heads, HD), jnp.float32),
            pltpu.VMEM((2, nb, features), jnp.bfloat16),
            sems, sems, sems, sems, sems, sems,
            pltpu.SemaphoreType.DMA((nb,)),
            pltpu.SemaphoreType.DMA((nb,)),
        ],
        compiler_params=pltpu.CompilerParams(
            collective_id=0, has_side_effects=True, vmem_limit_bytes=56 * 2**20
        ),
        name="bar_attention",
    )(bar_lengths, queries, keys, values)


def solution(mesh):
    placed = (
        P(("groups", "ctx"), None),
        P(("groups", "ctx"), None),
        P(("groups", "ctx"), None),
        P("groups"),
    )
    return jax.shard_map(
        local, mesh=mesh, in_specs=placed, out_specs=P(("groups", "ctx"), None), check_vma=False
    )
```

time: 365 us -> 169 us (0.46); the launches traced: 358 us -> 168 us
  blocking collectives: 244 us -> 0 us
  Pallas kernels: 0 us -> 166 us
  local copies, waits for them, and re-layouts: 67.8 us -> 2.3 us
  matrix products: 27.5 us -> 0 us
  starting transfers between devices: 9.21 us -> 0 us
  other arithmetic: 5.7 us -> 0 us
  between operations: 4.11 us -> 0.01 us
    all_gather x2 -> x0, blocking collectives: 244 us -> none  [the longest x1 228 us: local(): lax.all_gather(pooled_values, 'ctx', axis=0, tiled=True)]
    pallas_call x0 -> x1, Pallas kernels: none -> 166 us  [local(): pl.pallas_call(functools.partial(kernel, nb, hops, chunks), out_shape=jax...]
    concatenate x15 -> x0, local copies, waits for them, and re-layouts: 25 us -> none  [the longest x7 13.3 us: local(): key_rows = jnp.concatenate(key_parts, 0).reshape(-1, head_count, HD)]
    unnamed x49 -> x1, local copies, waits for them, and re-layouts: 26 us -> 2.3 us
    sub x1 -> x0, matrix products: 16.2 us -> none  [local(): weights = jnp.where(key_mask[None], jnp.exp(scores - row_max), 0.0)]
    slice x5 -> x0, local copies, waits for them, and re-layouts: 14.7 us -> none  [local(): key_parts.append(arrived[0])]
    dot_general x3 -> x0, matrix products: 11.4 us -> none  [the longest x1 8.98 us: local(): jnp.einsum('hqk,khd->qhd', rounded, value_rows, preferred_element_type=jn...]
    ppermute x5 -> x0, starting transfers between devices: 9.21 us -> none  [from_behind(): lax.ppermute(value, axis, [(source, source + steps) for source in range(i...]
  transfers between devices with their start and end apart: 5 -> 0, of which waited for: 0 -> 0; matrix products, arithmetic and copies ran while one was open for 11% -> 0% of each run, Pallas kernels for 0% -> 0%
where the time goes in v1:
time: 169 us; the launch traced here: 168 us
  Pallas kernels  166 us (98%)
  local copies, waits for them, and re-layouts  2.3 us (1%)
    pallas_call x1, Pallas kernels, local(): pl.pallas_call(functools.partial(kernel, nb, hops, chunks), out_shape=jax...  166 us

profile of v1, /device:TPU:26, one launch (start us, length us, event | category | flops | bytes accessed | tf_op | source)
XLA Modules:
  0.0 168.5 jit_solution(11838021648300636306)
XLA Ops:
  0.0 166.1 %bar_attention.1 = bf16[256,2048]{1,0:T(8,128)(2,1)} custom-call(s32[16]{0:T(128)} %len_ref.1, bf16[256,2048]{1,0:T(8,128)(2,1)} %q_ref.1, bf16[256,2048]{1,0:T(8,128)(2,1)} %k_ref.1, bf16[256,2048]{1,0:T(8,128)(2,1)} %v_ref.1), custom_call_target="tpu_custom_call" | custom-call | tf_op jit(solution)/shard_map/bar_attention/pallas_call | solution.py:367
  166.2 2.3 %copy.6 = bf16[256,2048]{1,0:T(8,128)(2,1)} copy(bf16[256,2048]{1,0:T(8,128)(2,1)} %bar_attention.1) | data formatting | bytes 2097152

commit v2 on v1

--- a/solution.py
+++ b/solution.py
@@ -13,14 +13,18 @@
 NEG_FILL = -1e30
 LOG2E = math.log2(math.e)
 SCALE = LOG2E / math.sqrt(HD)
-CHUNKS = 4
-AHEAD = 1
+CHUNKS = 8
+EARLY = 1
+LAG_NEAR = 1
+LAG_EDGE = 2
+LAG_FAR = 2
+LAG_HOP = 1
 STRIDE = 4
 
 
 def kernel(
     nb, hops, chunks, len_ref, q_ref, k_ref, v_ref, o_ref,
-    qin, oin, osend, lin, lsend, acc, mst, lst, sum_f32, sum_send, sum_in, sum_wide, sum_rows,
+    qin, oin, osend, lin, lloc, held, acc, sum_f32, sum_send, sum_in, sum_wide, sum_rows,
     q_send, q_recv, o_send, o_recv, l_send, l_recv, s_send, s_recv,
 ):
     rows, features = q_ref.shape
@@ -29,6 +33,7 @@
     per = width // HD
     near2, near1 = hops, hops + 1
     slots = hops + 2
+    own, own_held = slots, hops - 1
     me = lax.axis_index("ctx")
     low_half = lax.rem(lax.div(me, 2), 2) == 0
     even = lax.rem(me, 2) == 0
@@ -61,7 +66,7 @@
                 device_id_type=pl.DeviceIdType.MESH,
             ),
             pltpu.make_async_remote_copy(
-                src_ref=lsend.at[slot, c], dst_ref=lin.at[slot, c], send_sem=l_send.at[slot, c],
+                src_ref=lloc.at[slot, c], dst_ref=lin.at[slot, c], send_sem=l_send.at[slot, c],
                 recv_sem=l_recv.at[slot, c], device_id={"ctx": target},
                 device_id_type=pl.DeviceIdType.MESH,
             ),
@@ -97,8 +102,8 @@
 
     pl.semaphore_wait(barrier, nb - 1)
 
-    for c in range(chunks):
-        source = q_ref.at[:, c * width : (c + 1) * width]
+    def send_own(c):
+        source = q_ref.at[:, columns(c)]
 
         @pl.when(me >= STRIDE)
         def _():
@@ -112,12 +117,14 @@
         def _():
             q_copy(source, near1, c, me - 1).start()
 
-        if c == 0:
-            @pl.loop(0, nb)
-            def _(j):
-                @pl.when(j > me)
-                def _():
-                    s_copy(j).start()
+    for c in range(min(EARLY, chunks)):
+        send_own(c)
+
+    @pl.loop(0, nb)
+    def _(j):
+        @pl.when(j > me)
+        def _():
+            s_copy(j).start()
 
     def forward(c):
         for slot in range(slots):
@@ -137,6 +144,11 @@
                     def _():
                         q_copy(qin.at[slot, c], near1, c, me + 1).start()
 
+            if slot == hops - 1:
+                @pl.when(c + EARLY < chunks)
+                def _():
+                    send_own(c + EARLY)
+
     lane = lax.broadcasted_iota(jnp.int32, (rows, HD), 1)
     key_pos = lax.broadcasted_iota(jnp.int32, (1, rows), 1)
     live_bias = jnp.where(key_pos < own_len, 0.0, NEG_FILL).astype(jnp.float32)
@@ -148,6 +160,14 @@
 
     def head_columns(c, h):
         return pl.ds(pl.multiple_of(c * width + h * HD, HD), HD)
+
+    def keep_state(levels, totals, slot, c):
+        inverse = 1.0 / totals
+        for h in range(per):
+            here = slice(h * HD, (h + 1) * HD)
+            acc[:, here] = acc[:, here] * inverse[:, h : h + 1]
+        log_sums = levels + jnp.log(totals) * LOG2E
+        lloc[slot, c] = jnp.transpose(log_sums)[: lloc.shape[2], :]
 
     def local_peer(slot, c):
         m_all = jnp.zeros((rows, HD), jnp.float32)
@@ -164,8 +184,7 @@
             )
             m_all = jnp.where(lane == h, m, m_all)
             l_all = jnp.where(lane == h, l, l_all)
-        mst[...] = m_all
-        lst[...] = l_all
+        keep_state(m_all, l_all, slot, c)
 
     def local_own(c):
         causal = (
@@ -199,40 +218,50 @@
             )
             m_all = jnp.where(lane == h, m, m_all)
             l_all = jnp.where(lane == h, l, l_all)
-        mst[...] = m_all
-        lst[...] = l_all
-
-    def merge(slot, c):
-        for copy in o_copies(slot, c, parent(slot)):
+        keep_state(m_all, l_all, own, c)
+        held[own_held, c] = acc[...]
+
+    def merge(child, held_slot, slot, c):
+        for copy in o_copies(child, c, parent(child)):
             copy.wait_recv()
-        padded = jnp.concatenate(
-            [lin[slot, c], jnp.zeros((HD - lin.shape[2], rows), jnp.float32)], axis=0
+        mine, theirs = lloc[slot, c], lin[child, c]
+        top = jnp.maximum(mine, theirs)
+        both = top + jnp.log(jnp.exp2(mine - top) + jnp.exp2(theirs - top)) * LOG2E
+        lloc[slot, c] = both
+        shares = jnp.transpose(
+            jnp.concatenate(
+                [
+                    jnp.exp2(mine - both),
+                    jnp.exp2(theirs - both),
+                    jnp.zeros((HD - 2 * mine.shape[0], rows), jnp.float32),
+                ],
+                axis=0,
+            )
         )
-        theirs = jnp.transpose(padded)
-        mine = mst[...]
-        top = jnp.maximum(mine, theirs)
-        keep = jnp.exp2(mine - top)
-        add = jnp.exp2(theirs - top)
-        mst[...] = top
-        lst[...] = lst[...] * keep + add
+        second = mine.shape[0]
         for h in range(per):
             here = slice(h * HD, (h + 1) * HD)
-            acc[:, here] = (
-                acc[:, here] * keep[:, h : h + 1]
-                + oin[slot, c, :, here].astype(jnp.float32) * add[:, h : h + 1]
-            )
+            held[held_slot, c, :, here] = (
+                held[held_slot, c, :, here] * shares[:, h : h + 1]
+                + oin[child, c, :, here].astype(jnp.float32) * shares[:, second + h : second + h + 1]
+            )
+
+    def send_state(state, slot, c):
+        osend[slot, c] = state.astype(jnp.bfloat16)
+        for copy in o_copies(slot, c, parent(slot)):
+            copy.start()
 
     idle_hops = [s for s in range(hops) if STRIDE * (s + 1) not in BAR_OFFSETS]
-
-    def answer(slot, c):
+    far_child = me >= STRIDE
+
+    def local_answer(slot, c):
         if idle_hops:
             idle = functools.reduce(jnp.logical_or, [slot == s for s in idle_hops])
 
             @pl.when(idle)
             def _():
                 acc[...] = jnp.zeros_like(acc)
-                mst[...] = jnp.full_like(mst, NEG_FILL)
-                lst[...] = jnp.ones_like(lst)
+                lloc[slot, c] = jnp.full(lloc.shape[2:], NEG_FILL, jnp.float32)
 
             @pl.when(jnp.logical_not(idle))
             def _():
@@ -240,52 +269,37 @@
         else:
             local_peer(slot, c)
 
-        @pl.when((slot + 1 < hops) & (me >= STRIDE))
-        def _():
-            merge(jnp.minimum(slot + 1, hops - 1), c)
-
-        @pl.when((slot == 0) & low_half)
-        def _():
-            merge(near2, c)
-
-        @pl.when((slot == near2) & even)
-        def _():
-            merge(near1, c)
-
-        total = lst[...]
-        inverse = 1.0 / total
+        has_child = (
+            ((slot + 1 < hops) & far_child) | ((slot == 0) & low_half) | ((slot == near2) & even)
+        )
+
+        @pl.when(jnp.logical_not(has_child))
+        def _():
+            send_state(acc[...], slot, c)
+
+        @pl.when(has_child)
+        def _():
+            held[slot, c] = acc[...]
+
+    def finish(c):
+        @pl.when(far_child)
+        def _():
+            merge(0, own_held, own, c)
+
+        @pl.when(jnp.logical_not(low_half))
+        def _():
+            merge(near2, own_held, own, c)
+
+        @pl.when(jnp.logical_not(even))
+        def _():
+            merge(near1, own_held, own, c)
+
+        used = lax.broadcasted_iota(jnp.int32, (rows, HD), 0) < own_len
         for h in range(per):
             here = slice(h * HD, (h + 1) * HD)
-            osend[slot, c, :, here] = (acc[:, here] * inverse[:, h : h + 1]).astype(jnp.bfloat16)
-        level = mst[...] + jnp.log(total) * LOG2E
-        lsend[slot, c] = jnp.transpose(level)[: lsend.shape[2], :]
-        for copy in o_copies(slot, c, parent(slot)):
-            copy.start()
-
-    def finish(c):
-        local_own(c)
-
-        @pl.when(me >= STRIDE)
-        def _():
-            merge(0, c)
-
-        @pl.when(jnp.logical_not(low_half))
-        def _():
-            merge(near2, c)
-
-        @pl.when(jnp.logical_not(even))
-        def _():
-            merge(near1, c)
-
-        used = lax.broadcasted_iota(jnp.int32, (rows, HD), 0) < own_len
-        inverse = jnp.where(used, 1.0 / lst[...], 0.0)
-        for h in range(per):
-            o_ref[:, head_columns(c, h)] = (
-                acc[:, h * HD : (h + 1) * HD] * inverse[:, h : h + 1]
+            o_ref[:, head_columns(c, h)] = jnp.where(
+                used, held[own_held, c, :, here], 0.0
             ).astype(o_ref.dtype)
-
-    for c in range(min(AHEAD, chunks)):
-        forward(c)
 
     @pl.loop(0, nb)
     def _(j):
@@ -304,13 +318,23 @@
                 jnp.bfloat16
             )
 
-    @pl.loop(0, chunks + 1)
+    far_lags = [LAG_FAR + LAG_HOP * (hops - 2 - s) for s in range(hops - 1)]
+    own_lag = (far_lags[0] if far_lags else LAG_FAR) + LAG_HOP
+
+    @pl.loop(0, chunks + 1 + own_lag)
     def _(step):
-        @pl.when(step + AHEAD < chunks)
-        def _():
-            forward(step + AHEAD)
+        def at(lag, also, body):
+            c = step - 1 - lag
+
+            @pl.when((c >= 0) & (c < chunks) & also)
+            def _():
+                body(c)
 
         @pl.when(step < chunks)
+        def _():
+            forward(step)
+
+        @pl.when((step >= 1) & (step <= chunks))
         def _():
             @pl.loop(0, slots)
             def _(j):
@@ -318,11 +342,36 @@
 
                 @pl.when(exists(slot))
                 def _():
-                    answer(slot, step)
-
-        @pl.when(step >= 1)
-        def _():
-            finish(step - 1)
+                    local_answer(slot, step - 1)
+
+            local_own(step - 1)
+
+        def near_answer(c):
+            merge(near1, near2, near2, c)
+            send_state(held[near2, c], near2, c)
+
+        at(LAG_NEAR, exists(near2) & even, near_answer)
+
+        for s in reversed(range(hops)):
+            def far_answer(c, s=s):
+                merge(s + 1, s, s, c)
+                if s == 0:
+                    @pl.when(low_half)
+                    def _():
+                        merge(near2, s, s, c)
+                send_state(held[s, c], s, c)
+
+            def edge_answer(c):
+                merge(near2, 0, 0, c)
+                send_state(held[0, c], 0, c)
+
+            if s < hops - 1:
+                at(far_lags[s], exists(s) & far_child, far_answer)
+            if s == 0:
+                alone = low_half if hops == 1 else low_half & jnp.logical_not(far_child)
+                at(LAG_EDGE, exists(0) & alone, edge_answer)
+
+        at(own_lag, me >= 0, finish)
 
     @pl.loop(0, nb)
     def _(j):
@@ -374,10 +423,9 @@
             pltpu.VMEM(piece, jnp.bfloat16),
             pltpu.VMEM(piece, jnp.bfloat16),
             pltpu.VMEM((slots, chunks, stat_rows, rows), jnp.float32),
-            pltpu.VMEM((slots, chunks, stat_rows, rows), jnp.float32),
+            pltpu.VMEM((slots + 1, chunks, stat_rows, rows), jnp.float32),
+            pltpu.VMEM((hops + 1, chunks, rows, width), jnp.float32),
             pltpu.VMEM((rows, width), jnp.float32),
-            pltpu.VMEM((rows, HD), jnp.float32),
-            pltpu.VMEM((rows, HD), jnp.float32),
             pltpu.VMEM((2 * heads, HD), jnp.float32),
             pltpu.VMEM((2 * heads, HD), jnp.bfloat16),
             pltpu.VMEM((nb, 2 * heads, HD), jnp.bfloat16),
@@ -388,7 +436,7 @@
             pltpu.SemaphoreType.DMA((nb,)),
         ],
         compiler_params=pltpu.CompilerParams(
-            collective_id=0, has_side_effects=True, vmem_limit_bytes=56 * 2**20
+            collective_id=0, has_side_effects=True, vmem_limit_bytes=60 * 2**20
         ),
         name="bar_attention",
     )(bar_lengths, queries, keys, values)

time: 169 us -> 119 us (0.70)
  the two profiles are of different devices: /device:TPU:26 before, /device:TPU:21 now
where the time goes in v2:
time: 119 us
  Pallas kernels  117 us (98%)
  local copies, waits for them, and re-layouts  2.3 us (2%)
    pallas_call x1, Pallas kernels, local(): pl.pallas_call(functools.partial(kernel, nb, hops, chunks), out_shape=jax...  117 us

profile of v2, /device:TPU:21, one launch (start us, length us, event | category | flops | bytes accessed | tf_op | source)
XLA Modules:
  0.0 119.3 jit_solution(5479595780333752937)
XLA Ops:
  0.0 117.0 %bar_attention.1 = bf16[256,2048]{1,0:T(8,128)(2,1)} custom-call(s32[16]{0:T(128)} %len_ref.1, bf16[256,2048]{1,0:T(8,128)(2,1)} %q_ref.1, bf16[256,2048]{1,0:T(8,128)(2,1)} %k_ref.1, bf16[256,2048]{1,0:T(8,128)(2,1)} %v_ref.1), custom_call_target="tpu_custom_call" | custom-call | tf_op jit(solution)/shard_map/bar_attention/pallas_call | solution.py:416
  117.0 2.3 %copy.6 = bf16[256,2048]{1,0:T(8,128)(2,1)} copy(bf16[256,2048]{1,0:T(8,128)(2,1)} %bar_attention.1) | data formatting | bytes 2097152

commit v3 on v2

--- a/solution.py
+++ b/solution.py
@@ -24,8 +24,8 @@
 
 def kernel(
     nb, hops, chunks, len_ref, q_ref, k_ref, v_ref, o_ref,
-    qin, oin, osend, lin, lloc, held, acc, sum_f32, sum_send, sum_in, sum_wide, sum_rows,
-    q_send, q_recv, o_send, o_recv, l_send, l_recv, s_send, s_recv,
+    qin, oin, osend, lin, lloc, held, acc, low_kv, sum_f32, sum_send, sum_in, sum_wide, sum_rows,
+    q_send, q_recv, o_send, o_recv, l_send, l_recv, s_send, s_recv, kv_send, kv_recv,
 ):
     rows, features = q_ref.shape
     heads = features // HD
@@ -33,41 +33,47 @@
     per = width // HD
     near2, near1 = hops, hops + 1
     slots = hops + 2
-    own, own_held = slots, hops - 1
+    own, own_held, extra = slots, hops - 1, slots
     me = lax.axis_index("ctx")
     low_half = lax.rem(lax.div(me, 2), 2) == 0
     even = lax.rem(me, 2) == 0
     own_len = len_ref[me]
+    lender = me < STRIDE
+    borrower = (me >= STRIDE) & (me < 2 * STRIDE)
+    inner = me >= 2 * STRIDE
+    direct = lender & jnp.logical_not(low_half)
 
     def columns(c):
         return pl.ds(pl.multiple_of(c * width, width), width)
 
     def exists(slot):
-        far = me + STRIDE * (slot + 1) < nb
+        far = (me + STRIDE * (slot + 1) < nb) & jnp.logical_not(lender)
         return jnp.where(slot == near2, me + 2 < nb, jnp.where(slot == near1, me + 1 < nb, far))
 
     def parent(slot):
-        two = jnp.where(low_half, me + 2, me - 2)
+        two = jnp.where(low_half | direct, me + 2, me - 2)
         one = jnp.where(even, me + 1, me - 1)
         return jnp.where(slot == near2, two, jnp.where(slot == near1, one, me + STRIDE))
 
-    def q_copy(src, slot, c, target):
+    def q_copy(src, slot, c, target, lane=None):
         return pltpu.make_async_remote_copy(
-            src_ref=src, dst_ref=qin.at[slot, c], send_sem=q_send.at[slot, c],
+            src_ref=src, dst_ref=qin.at[slot, c], send_sem=q_send.at[slot if lane is None else lane, c],
             recv_sem=q_recv.at[slot, c], device_id={"ctx": target},
             device_id_type=pl.DeviceIdType.MESH,
         )
 
-    def o_copies(slot, c, target):
+    def o_copies(slot, c, target, into=None):
+        if into is None:
+            into = jnp.where((slot == near2) & direct, extra, slot)
         return (
             pltpu.make_async_remote_copy(
-                src_ref=osend.at[slot, c], dst_ref=oin.at[slot, c], send_sem=o_send.at[slot, c],
-                recv_sem=o_recv.at[slot, c], device_id={"ctx": target},
+                src_ref=osend.at[slot, c], dst_ref=oin.at[into, c], send_sem=o_send.at[slot, c],
+                recv_sem=o_recv.at[into, c], device_id={"ctx": target},
                 device_id_type=pl.DeviceIdType.MESH,
             ),
             pltpu.make_async_remote_copy(
-                src_ref=lloc.at[slot, c], dst_ref=lin.at[slot, c], send_sem=l_send.at[slot, c],
-                recv_sem=l_recv.at[slot, c], device_id={"ctx": target},
+                src_ref=lloc.at[slot, c], dst_ref=lin.at[into, c], send_sem=l_send.at[slot, c],
+                recv_sem=l_recv.at[into, c], device_id={"ctx": target},
                 device_id_type=pl.DeviceIdType.MESH,
             ),
         )
@@ -102,12 +108,31 @@
 
     pl.semaphore_wait(barrier, nb - 1)
 
+    def kv_copies(c):
+        return [
+            pltpu.make_async_remote_copy(
+                src_ref=ref.at[:, columns(c)], dst_ref=low_kv.at[part, c],
+                send_sem=kv_send.at[part, c], recv_sem=kv_recv.at[part, c],
+                device_id={"ctx": me + STRIDE}, device_id_type=pl.DeviceIdType.MESH,
+            )
+            for part, ref in enumerate((k_ref, v_ref))
+        ]
+
     def send_own(c):
         source = q_ref.at[:, columns(c)]
 
-        @pl.when(me >= STRIDE)
+        @pl.when(inner)
         def _():
             q_copy(source, 0, c, me - STRIDE).start()
+
+        @pl.when(borrower & low_half)
+        def _():
+            q_copy(source, near2, c, me - 2, extra).start()
+
+        @pl.when(lender)
+        def _():
+            for copy in kv_copies(c):
+                copy.start()
 
         @pl.when(jnp.logical_not(low_half))
         def _():
@@ -132,7 +157,7 @@
             def _(slot=slot):
                 q_copy(qin.at[slot, c], slot, c, parent(slot)).wait_recv()
                 if slot + 1 < hops:
-                    @pl.when(me >= STRIDE)
+                    @pl.when(inner)
                     def _():
                         q_copy(qin.at[slot, c], slot + 1, c, me - STRIDE).start()
                 if slot == 0:
@@ -152,6 +177,12 @@
     lane = lax.broadcasted_iota(jnp.int32, (rows, HD), 1)
     key_pos = lax.broadcasted_iota(jnp.int32, (1, rows), 1)
     live_bias = jnp.where(key_pos < own_len, 0.0, NEG_FILL).astype(jnp.float32)
+
+    low_len = len_ref[jnp.maximum(me - STRIDE, 0)]
+    low_bias = jnp.where(key_pos < low_len, 0.0, NEG_FILL).astype(jnp.float32)
+
+    def listed(distance):
+        return functools.reduce(jnp.logical_or, [distance == o for o in BAR_OFFSETS])
 
     def scores_of(q, k):
         return lax.dot_general(
@@ -186,7 +217,32 @@
             l_all = jnp.where(lane == h, l, l_all)
         keep_state(m_all, l_all, slot, c)
 
-    def local_own(c):
+    def local_two(slot, c):
+        near_bias = live_bias + jnp.where(listed(STRIDE * (slot + 1)), 0.0, NEG_FILL)
+        far_bias = low_bias + jnp.where(listed(STRIDE * (slot + 2)), 0.0, NEG_FILL)
+        m_all = jnp.zeros((rows, HD), jnp.float32)
+        l_all = jnp.ones((rows, HD), jnp.float32)
+        for h in range(per):
+            here = slice(h * HD, (h + 1) * HD)
+            q = qin[slot, c, :, here]
+            s = scores_of(q, k_ref[:, head_columns(c, h)]) + near_bias
+            t = scores_of(q, low_kv[0, c, :, here]) + far_bias
+            m = jnp.max(jnp.maximum(s, t), axis=1, keepdims=True)
+            p = jnp.exp2(s - m)
+            r = jnp.exp2(t - m)
+            l = jnp.sum(p + r, axis=1, keepdims=True)
+            acc[:, here] = jnp.dot(
+                p.astype(jnp.bfloat16), v_ref[:, head_columns(c, h)],
+                preferred_element_type=jnp.float32,
+            ) + jnp.dot(
+                r.astype(jnp.bfloat16), low_kv[1, c, :, here],
+                preferred_element_type=jnp.float32,
+            )
+            m_all = jnp.where(lane == h, m, m_all)
+            l_all = jnp.where(lane == h, l, l_all)
+        keep_state(m_all, l_all, slot, c)
+
+    def local_own(c, two):
         causal = (
             lax.broadcasted_iota(jnp.int32, (rows, rows), 1)
             <= lax.broadcasted_iota(jnp.int32, (rows, rows), 0)
@@ -206,23 +262,34 @@
             m = jnp.maximum(
                 jnp.max(s, axis=1, keepdims=True), jnp.max(t, axis=1, keepdims=True)
             )
+            if two:
+                u = scores_of(q, low_kv[0, c, :, here]) + low_bias
+                m = jnp.maximum(m, jnp.max(u, axis=1, keepdims=True))
             p = jnp.exp2(s - m)
             r = jnp.exp2(t - m)
             l = jnp.sum(p, axis=1, keepdims=True) + jnp.sum(r, axis=1, keepdims=True)
-            acc[:, here] = jnp.dot(
+            mixed = jnp.dot(
                 p.astype(jnp.bfloat16), v_ref[:, head_columns(c, h)],
                 preferred_element_type=jnp.float32,
             ) + jnp.dot(
                 r.astype(jnp.bfloat16), sum_rows[1, :, head_columns(c, h)],
                 preferred_element_type=jnp.float32,
             )
+            if two:
+                w = jnp.exp2(u - m)
+                l = l + jnp.sum(w, axis=1, keepdims=True)
+                mixed = mixed + jnp.dot(
+                    w.astype(jnp.bfloat16), low_kv[1, c, :, here],
+                    preferred_element_type=jnp.float32,
+                )
+            acc[:, here] = mixed
             m_all = jnp.where(lane == h, m, m_all)
             l_all = jnp.where(lane == h, l, l_all)
         keep_state(m_all, l_all, own, c)
         held[own_held, c] = acc[...]
 
     def merge(child, held_slot, slot, c):
-        for copy in o_copies(child, c, parent(child)):
+        for copy in o_copies(min(child, near1), c, parent(min(child, near1)), child):
             copy.wait_recv()
         mine, theirs = lloc[slot, c], lin[child, c]
         top = jnp.maximum(mine, theirs)
@@ -252,22 +319,31 @@
             copy.start()
 
     idle_hops = [s for s in range(hops) if STRIDE * (s + 1) not in BAR_OFFSETS]
-    far_child = me >= STRIDE
+    far_child = inner
 
     def local_answer(slot, c):
+        double = borrower & (slot < hops)
+
+        @pl.when(double)
+        def _():
+            local_two(slot, c)
+
         if idle_hops:
             idle = functools.reduce(jnp.logical_or, [slot == s for s in idle_hops])
+            idle = idle & jnp.logical_not(double)
 
             @pl.when(idle)
             def _():
                 acc[...] = jnp.zeros_like(acc)
                 lloc[slot, c] = jnp.full(lloc.shape[2:], NEG_FILL, jnp.float32)
 
-            @pl.when(jnp.logical_not(idle))
+            @pl.when(jnp.logical_not(idle | double))
             def _():
                 local_peer(slot, c)
         else:
-            local_peer(slot, c)
+            @pl.when(jnp.logical_not(double))
+            def _():
+                local_peer(slot, c)
 
         has_child = (
             ((slot + 1 < hops) & far_child) | ((slot == 0) & low_half) | ((slot == near2) & even)
@@ -293,6 +369,10 @@
         @pl.when(jnp.logical_not(even))
         def _():
             merge(near1, own_held, own, c)
+
+        @pl.when(borrower & low_half)
+        def _():
+            merge(extra, own_held, own, c)
 
         used = lax.broadcasted_iota(jnp.int32, (rows, HD), 0) < own_len
         for h in range(per):
@@ -336,6 +416,11 @@
 
         @pl.when((step >= 1) & (step <= chunks))
         def _():
+            @pl.when(borrower)
+            def _():
+                for copy in kv_copies(step - 1):
+                    copy.wait_recv()
+
             @pl.loop(0, slots)
             def _(j):
                 slot = slots - 1 - j
@@ -344,7 +429,13 @@
                 def _():
                     local_answer(slot, step - 1)
 
-            local_own(step - 1)
+            @pl.when(borrower)
+            def _():
+                local_own(step - 1, True)
+
+            @pl.when(jnp.logical_not(borrower))
+            def _():
+                local_own(step - 1, False)
 
         def near_answer(c):
             merge(near1, near2, near2, c)
@@ -381,13 +472,22 @@
 
     @pl.loop(0, chunks)
     def _(c):
+        @pl.when(borrower & low_half)
+        def _():
+            q_copy(qin.at[near2, c], near2, c, me - 2, extra).wait_send()
+
+        @pl.when(lender)
+        def _():
+            for copy in kv_copies(c):
+                copy.wait_send()
+
         for slot in range(slots):
             if slot == 0:
-                sent = me >= STRIDE
+                sent = inner
             elif slot < hops:
-                sent = (me >= STRIDE) & (me + STRIDE * slot < nb)
+                sent = inner & (me + STRIDE * slot < nb)
             elif slot == near2:
-                sent = jnp.logical_not(low_half) | (me + STRIDE < nb)
+                sent = jnp.logical_not(low_half) | ((me + STRIDE < nb) & jnp.logical_not(lender))
             else:
                 sent = jnp.logical_not(even) | (me + 2 < nb)
 
@@ -408,10 +508,11 @@
     chunks = CHUNKS
     width = features // chunks
     hops = max(o // STRIDE for o in BAR_OFFSETS if o % STRIDE == 0 and o < nb)
+    hops = min(hops, nb // STRIDE - 2)
     slots = hops + 2
     stat_rows = 8
     piece = (slots, chunks, rows, width)
-    sems = pltpu.SemaphoreType.DMA((slots, chunks))
+    sems = pltpu.SemaphoreType.DMA((slots + 1, chunks))
     whole = pl.BlockSpec(memory_space=pltpu.VMEM)
     return pl.pallas_call(
         functools.partial(kernel, nb, hops, chunks),
@@ -420,12 +521,13 @@
         out_specs=whole,
         scratch_shapes=[
             pltpu.VMEM(piece, jnp.bfloat16),
+            pltpu.VMEM((slots + 1,) + piece[1:], jnp.bfloat16),
             pltpu.VMEM(piece, jnp.bfloat16),
-            pltpu.VMEM(piece, jnp.bfloat16),
-            pltpu.VMEM((slots, chunks, stat_rows, rows), jnp.float32),
+            pltpu.VMEM((slots + 1, chunks, stat_rows, rows), jnp.float32),
             pltpu.VMEM((slots + 1, chunks, stat_rows, rows), jnp.float32),
             pltpu.VMEM((hops + 1, chunks, rows, width), jnp.float32),
             pltpu.VMEM((rows, width), jnp.float32),
+            pltpu.VMEM((2, chunks, rows, width), jnp.bfloat16),
             pltpu.VMEM((2 * heads, HD), jnp.float32),
             pltpu.VMEM((2 * heads, HD), jnp.bfloat16),
             pltpu.VMEM((nb, 2 * heads, HD), jnp.bfloat16),
@@ -434,6 +536,8 @@
             sems, sems, sems, sems, sems, sems,
             pltpu.SemaphoreType.DMA((nb,)),
             pltpu.SemaphoreType.DMA((nb,)),
+            pltpu.SemaphoreType.DMA((2, chunks)),
+            pltpu.SemaphoreType.DMA((2, chunks)),
         ],
         compiler_params=pltpu.CompilerParams(
             collective_id=0, has_side_effects=True, vmem_limit_bytes=60 * 2**20

time: 119 us -> 112 us (0.941)
  the two profiles are of different devices: /device:TPU:21 before, /device:TPU:26 now
where the time goes in v3:
time: 112 us
  Pallas kernels  110 us (98%)
  local copies, waits for them, and re-layouts  2.3 us (2%)
    pallas_call x1, Pallas kernels, local(): pl.pallas_call(functools.partial(kernel, nb, hops, chunks), out_shape=jax...  110 us
    unnamed x1, local copies, waits for them, and re-layouts  2.3 us

profile of v3, /device:TPU:26, one launch (start us, length us, event | category | flops | bytes accessed | tf_op | source)
XLA Modules:
  0.0 112.0 jit_solution(12447448571888057126)
XLA Ops:
  0.0 109.6 %bar_attention.1 = bf16[256,2048]{1,0:T(8,128)(2,1)} custom-call(s32[16]{0:T(128)} %len_ref.1, bf16[256,2048]{1,0:T(8,128)(2,1)} %q_ref.1, bf16[256,2048]{1,0:T(8,128)(2,1)} %k_ref.1, bf16[256,2048]{1,0:T(8,128)(2,1)} %v_ref.1), custom_call_target="tpu_custom_call" | custom-call | tf_op jit(solution)/shard_map/bar_attention/pallas_call | solution.py:517
  109.7 2.3 %copy.6 = bf16[256,2048]{1,0:T(8,128)(2,1)} copy(bf16[256,2048]{1,0:T(8,128)(2,1)} %bar_attention.1) | data formatting | bytes 2097152

commit v4 on v3

--- a/solution.py
+++ b/solution.py
@@ -15,8 +15,9 @@
 SCALE = LOG2E / math.sqrt(HD)
 CHUNKS = 8
 EARLY = 1
-LAG_NEAR = 1
-LAG_EDGE = 2
+LEND_EARLY = 0
+LAG_NEAR = 0
+LAG_EDGE = 1
 LAG_FAR = 2
 LAG_HOP = 1
 STRIDE = 4
@@ -129,21 +130,25 @@
         def _():
             q_copy(source, near2, c, me - 2, extra).start()
 
+        @pl.when(jnp.logical_not(low_half))
+        def _():
+            q_copy(source, near2, c, me - 2).start()
+
+        @pl.when(jnp.logical_not(even))
+        def _():
+            q_copy(source, near1, c, me - 1).start()
+
+    def lend(c):
         @pl.when(lender)
         def _():
             for copy in kv_copies(c):
                 copy.start()
 
-        @pl.when(jnp.logical_not(low_half))
-        def _():
-            q_copy(source, near2, c, me - 2).start()
-
-        @pl.when(jnp.logical_not(even))
-        def _():
-            q_copy(source, near1, c, me - 1).start()
-
     for c in range(min(EARLY, chunks)):
         send_own(c)
+
+    for c in range(min(LEND_EARLY, chunks)):
+        lend(c)
 
     @pl.loop(0, nb)
     def _(j):
@@ -173,6 +178,10 @@
                 @pl.when(c + EARLY < chunks)
                 def _():
                     send_own(c + EARLY)
+
+                @pl.when(c + LEND_EARLY < chunks)
+                def _():
+                    lend(c + LEND_EARLY)
 
     lane = lax.broadcasted_iota(jnp.int32, (rows, HD), 1)
     key_pos = lax.broadcasted_iota(jnp.int32, (1, rows), 1)

time: 112 us -> 104 us (0.929)
  Pallas kernels: 110 us -> 102 us
    pallas_call x1, Pallas kernels: 110 us -> 102 us  [local(): pl.pallas_call(functools.partial(kernel, nb, hops, chunks), out_shape=jax...]
where the time goes in v4:
time: 104 us
  Pallas kernels  102 us (98%)
  local copies, waits for them, and re-layouts  2.3 us (2%)
    pallas_call x1, Pallas kernels, local(): pl.pallas_call(functools.partial(kernel, nb, hops, chunks), out_shape=jax...  102 us
    unnamed x1, local copies, waits for them, and re-layouts  2.3 us

profile of v4, /device:TPU:26, one launch (start us, length us, event | category | flops | bytes accessed | tf_op | source)
XLA Modules:
  0.0 104.2 jit_solution(1623580151806177688)
XLA Ops:
  0.0 101.9 %bar_attention.1 = bf16[256,2048]{1,0:T(8,128)(2,1)} custom-call(s32[16]{0:T(128)} %len_ref.1, bf16[256,2048]{1,0:T(8,128)(2,1)} %q_ref.1, bf16[256,2048]{1,0:T(8,128)(2,1)} %k_ref.1, bf16[256,2048]{1,0:T(8,128)(2,1)} %v_ref.1), custom_call_target="tpu_custom_call" | custom-call | tf_op jit(solution)/shard_map/bar_attention/pallas_call | solution.py:526
  101.9 2.3 %copy.6 = bf16[256,2048]{1,0:T(8,128)(2,1)} copy(bf16[256,2048]{1,0:T(8,128)(2,1)} %bar_attention.1) | data formatting | bytes 2097152
